TPU v7x, 32 devices: a whole 2x2x4 slice. The times are simulated.
32 devices in a mesh: seq: 4 (over x, core), head: 8 (over z, y).
Axes of the slice: x: 2, y: 2, z: 4, core: 2. Of those that a mesh axis runs over, the one named last changes fastest.
Arguments:
- queries: bfloat16 [512, 8192], P('seq', 'head'), may hold values from -256 to 256
- key_rows: bfloat16 [512, 128], P('seq'), may hold values from -6 to 6
- value_rows: bfloat16 [512, 128], P('seq'), may hold values from -6 to 6
- pair_keys: bfloat16 [512, 128], P('seq'), may hold values from 0.27 to 1.73
- pair_values: bfloat16 [512, 128], P('seq'), may hold values from 0.099609375 to 1.8984375
- first_key: int32 [512], P('seq'), may hold values from 0 to 511, as said below
- residual: float32 [512, 8192], P(('seq', 'head')), may hold values from -6 to 6
- out_weight: bfloat16 [8192, 8192], P('head', 'seq'), may hold values from -0.25 to 0.25
Outputs:
- updated: float32 [512, 8192], P(('seq', 'head'))
Inputs may be any that keep to these rules, and one draw needn't show every extreme that they name: first_key never falls along the tokens, first_key[i] <= i, and first_key[i] = i where a document begins; positions 0 and 511 begin one.
All inputs are finite; a program needn't handle non-finite values.
Results may differ from a plain program's by a relative error of at most 0.005.
Values may be sent and summed in bfloat16 or wider, within the bound.
No kernel may reach another device: no remote copies, remote signals or barrier semaphores. Data moves between devices by JAX's collectives and lax.ppermute only.
A program may use at most 128 MiB of HBM per device.

v0:
```python
import functools
import math

import jax
import jax.numpy as jnp
from jax import lax
from jax.experimental import pallas as pl
from jax.experimental.pallas import tpu as pltpu
from jax.sharding import PartitionSpec as P

DH = 128
W1 = 512
W2 = 32
BLOCK = 128
LOW = -1e30
TILE = 8
GROUP = 4
GROUPS = 2
ROWS = TILE * W2


def attention_kernel(
    first_token, count, most, stride, own_ref, base_ref, first_ref, q_ref, ctx_ref, pk_ref, pv_ref,
    out_ref, qf, of, pkf, pk2, pvb, kx, vx, lhs, scores, weights,
):
    blocks = kx.shape[1] // BLOCK
    tok = pk_ref.shape[0]
    own = own_ref[0]
    base = base_ref[0]
    origin = base - own * tok
    per = tok // BLOCK
    for b in range(blocks):
        at = b // per * stride + b % per * BLOCK
        rows = slice(b * BLOCK, (b + 1) * BLOCK)
        for g in range(GROUPS):
            kx[g, rows, :DH] = ctx_ref[at : at + BLOCK, :DH]
        vx[rows, :DH] = ctx_ref[at : at + BLOCK, DH:]
        vx[rows, DH:] = jnp.ones((BLOCK, DH), jnp.bfloat16)
    if first_token == 0:
        before = pl.multiple_of(jnp.maximum(own - 1, 0) * stride + tok, W2)
        pkf[0:W2] = ctx_ref[pl.ds(before, W2)].astype(jnp.float32)
    else:
        pkf[0:W2, :DH] = pk_ref[first_token - W2 : first_token].astype(jnp.float32)
        pkf[0:W2, DH:] = pv_ref[first_token - W2 : first_token].astype(jnp.float32)
    pkf[W2 : W2 + count, :DH] = pk_ref[first_token : first_token + count].astype(jnp.float32)
    pkf[W2 : W2 + count, DH:] = pv_ref[first_token : first_token + count].astype(jnp.float32)
    pkf[W2 + count :] = jnp.zeros((8, 2 * DH), jnp.float32)

    def spread(blk, _):
        r0 = pl.multiple_of(blk * 8, 8)
        x = pkf[pl.ds(r0, 16)]
        for r in range(8):
            a = jnp.broadcast_to(x[r : r + 1, :DH], (TILE, DH))
            b = jnp.broadcast_to(x[r + 1 : r + 2, :DH], (TILE, DH))
            pk2[r0 + r] = jnp.concatenate([a, b], axis=0).astype(jnp.bfloat16)
            pvb[r0 + r] = jnp.broadcast_to(x[r : r + 1, DH:], (TILE, DH))
        return 0

    lax.fori_loop(0, (W2 + count) // 8, spread, 0)
    for h in range(TILE):
        qf[pl.ds(h, count, stride=TILE), :] = q_ref[
            first_token : first_token + count, h * DH : (h + 1) * DH
        ].astype(jnp.float32)
    unit = GROUP * ROWS
    row = lax.broadcasted_iota(jnp.int32, (unit, DH), 0)
    col = lax.broadcasted_iota(jnp.int32, (unit, DH), 1)
    pick = jnp.where(row // TILE == col, 1.0, 0.0).astype(jnp.bfloat16)
    for g in range(GROUPS):
        lhs[g * unit : (g + 1) * unit, DH:] = pick
    lane = lax.broadcasted_iota(jnp.int32, (1, DH), 1)
    lane_token = lane // W2
    lane_offset = lane % W2
    factor = math.log2(math.e) / math.sqrt(DH)
    tokens = GROUP * GROUPS

    def step(index, _):
        i0 = index * tokens
        pos0 = base + first_token + i0
        first = [first_ref[first_token + i0 + t] for t in range(tokens)]
        lowest = jnp.maximum(first[0], pos0 - W1 + 1)
        block_low = (lowest - origin) // BLOCK
        block_high = (pos0 + tokens - 1 - origin) // BLOCK
        start = pl.multiple_of(block_low * BLOCK, BLOCK)

        def run(n):
            keys = n * BLOCK
            key_pos = lax.broadcasted_iota(jnp.int32, (keys, DH), 0) + (origin + start)

            def score(g):
                mine = first[g * GROUP : (g + 1) * GROUP]
                first_lane = jnp.full((1, DH), mine[-1], jnp.int32)
                for t in range(GROUP - 2, -1, -1):
                    first_lane = jnp.where(lane_token == t, mine[t], first_lane)
                high = pos0 + g * GROUP + lane_token
                low = jnp.maximum(first_lane, high - W1 + 1)
                low = jnp.where(high - (W2 - 1) + lane_offset >= first_lane, low, 2**30)
                ok = (key_pos >= low) & (key_pos <= high)
                kx[g, pl.ds(start, keys), DH:] = jnp.where(ok, 0.0, LOW).astype(jnp.bfloat16)
                for t in range(g * GROUP, (g + 1) * GROUP):
                    q = qf[pl.ds(pl.multiple_of((i0 + t) * TILE, TILE), TILE)]
                    q = jnp.concatenate([q, q], axis=0).astype(jnp.bfloat16)
                    for k in range(W2 // 2):
                        at = t * ROWS + k * 16
                        lhs[at : at + 16, :DH] = q * pk2[i0 + t + 1 + 2 * k]
                scores[g * unit : (g + 1) * unit, :keys] = lax.dot_general(
                    lhs[g * unit : (g + 1) * unit],
                    kx[g, pl.ds(start, keys)],
                    (((1,), (1,)), ((), ())),
                    preferred_element_type=jnp.float32,
                )

            def soften(g):
                for t in range(g * GROUP, (g + 1) * GROUP):
                    rows = slice(t * ROWS, (t + 1) * ROWS)
                    s = scores[rows, :keys].reshape(W2, TILE, keys)
                    top = jnp.max(jnp.max(s, axis=0), axis=1, keepdims=True)
                    e = jnp.exp2((s - top[None]) * factor)
                    weights[rows, :keys] = e.reshape(ROWS, keys).astype(jnp.bfloat16)

            def value(g):
                o = jnp.dot(
                    weights[g * unit : (g + 1) * unit, :keys],
                    vx[pl.ds(start, keys)],
                    preferred_element_type=jnp.float32,
                )
                for t in range(GROUP):
                    carried = jnp.zeros((TILE, DH), jnp.float32)
                    total = jnp.zeros((TILE, DH), jnp.float32)
                    for w in range(W2):
                        at = t * ROWS + w * TILE
                        carried += o[at : at + TILE, :DH] * pvb[i0 + g * GROUP + t + 1 + w]
                        total += o[at : at + TILE, DH:]
                    at = pl.multiple_of((i0 + g * GROUP + t) * TILE, TILE)
                    of[pl.ds(at, TILE)] = carried / total

            score(0)
            for g in range(GROUPS):
                if g + 1 < GROUPS:
                    score(g + 1)
                soften(g)
                if g >= 1:
                    value(g - 1)
            value(GROUPS - 1)

        for n in range(1, most + 1):
            pl.when(block_high - block_low + 1 == n)(functools.partial(run, n))
        return 0

    lax.fori_loop(0, count // tokens, step, 0)
    for h in range(TILE):
        out_ref[:, h * DH : (h + 1) * DH] = of[pl.ds(h, count, stride=TILE), :].astype(jnp.bfloat16)


def attention(first_token, count, own, base, first_key, q, context, pair_keys, pair_values):
    tok = pair_keys.shape[0]
    stride = tok + W2
    rows = context.shape[0] // stride * tok
    most = min(rows // BLOCK, W1 // BLOCK + 1)
    f32, bf16 = jnp.float32, jnp.bfloat16
    unit = GROUPS * GROUP * ROWS
    return pl.pallas_call(
        functools.partial(attention_kernel, first_token, count, most, stride),
        out_shape=jax.ShapeDtypeStruct((count, TILE * DH), bf16),
        in_specs=[pl.BlockSpec(memory_space=pltpu.SMEM)] * 3
        + [pl.BlockSpec(memory_space=pltpu.VMEM)] * 4,
        out_specs=pl.BlockSpec(memory_space=pltpu.VMEM),
        scratch_shapes=[
            pltpu.VMEM((count * TILE, DH), f32),
            pltpu.VMEM((count * TILE, DH), f32),
            pltpu.VMEM((W2 + count + 8, 2 * DH), f32),
            pltpu.VMEM((W2 + count, 2 * TILE, DH), bf16),
            pltpu.VMEM((W2 + count, TILE, DH), f32),
            pltpu.VMEM((GROUPS, rows, 2 * DH), bf16),
            pltpu.VMEM((rows, 2 * DH), bf16),
            pltpu.VMEM((unit, 2 * DH), bf16),
            pltpu.VMEM((unit, most * BLOCK), f32),
            pltpu.VMEM((unit, most * BLOCK), bf16),
        ],
        compiler_params=pltpu.CompilerParams(vmem_limit_bytes=40 * 2**20),
        name="attention",
    )(own, base, first_key, q, context, pair_keys, pair_values)


def context_blocks(block, reach):
    count = lax.axis_size("seq")
    if count <= reach + 1:
        return lax.all_gather(block, "seq", axis=0, tiled=True), lax.axis_index("seq")
    pieces = [
        lax.ppermute(block, "seq", [(a, a + steps) for a in range(count - steps)])
        for steps in range(reach, 0, -1)
    ]
    return jnp.concatenate(pieces + [block], axis=0), jnp.int32(reach)


def gathered(value):
    count = lax.axis_size("seq")
    if count & (count - 1):
        return lax.all_gather(value, "seq", axis=0)
    me = lax.axis_index("seq")
    value = value[None]
    bit = count // 2
    while bit:
        other = lax.ppermute(value, "seq", [(a, a ^ bit) for a in range(count)])
        high = (me & bit) > 0
        first = jnp.where(high, other, value)
        second = jnp.where(high, value, other)
        value = jnp.stack([first, second], axis=1).reshape((-1,) + value.shape[1:])
        bit //= 2
    return value


def local(queries, key_rows, value_rows, pair_keys, pair_values, first_key, residual, out_weight):
    tok = queries.shape[0]
    width = queries.shape[1]
    seq_size, head_size = lax.axis_size("seq"), lax.axis_size("head")
    block = jnp.concatenate(
        [
            jnp.concatenate([key_rows, value_rows], axis=1),
            jnp.concatenate([pair_keys[tok - W2 :], pair_values[tok - W2 :]], axis=1),
        ],
        axis=0,
    )
    context, own = context_blocks(block, (W1 + tok - 1) // tok)
    base = lax.axis_index("seq") * tok
    own, base = (jnp.asarray(value, jnp.int32).reshape(1) for value in (own, base))
    tile = TILE * DH

    def attend(start, count):
        parts = []
        for at in range(0, width, tile):
            q = queries[:, at : at + tile]
            if q.shape[1] < tile:
                q = jnp.pad(q, ((0, 0), (0, tile - q.shape[1])))
            parts.append(
                attention(start, count, own, base, first_key, q, context, pair_keys, pair_values)
            )
        return (parts[0] if len(parts) == 1 else jnp.concatenate(parts, axis=1))[:, :width]

    columns = out_weight.shape[1]
    rows = tok // head_size
    every = gathered(attend(0, tok)).reshape(seq_size * tok, width)
    partial_rows = jnp.dot(every, out_weight, preferred_element_type=jnp.float32)
    sent = partial_rows.astype(jnp.bfloat16).reshape(seq_size * head_size, rows, columns)
    got = lax.all_to_all(sent, ("seq", "head"), 0, 0).reshape(seq_size, head_size, rows, columns)
    summed = jnp.sum(got.astype(jnp.float32), axis=1)
    return residual + jnp.swapaxes(summed, 0, 1).reshape(rows, seq_size * columns)


def solution(mesh):
    placed = (
        P("seq", "head"),
        P("seq", None),
        P("seq", None),
        P("seq", None),
        P("seq", None),
        P("seq"),
        P(("seq", "head"), None),
        P("head", "seq"),
    )
    return jax.shard_map(
        local, mesh=mesh, in_specs=placed, out_specs=P(("seq", "head"), None), check_vma=False
    )
```

profile of v0, /device:TPU:0, one launch (start us, length us, event | category | flops | bytes accessed | tf_op | source)
XLA Modules:
  0.0 105.1 jit_solution(13193899005120072917)
XLA Ops:
  0.0 0.7 slice.6
  0.7 0.7 slice.7
  1.4 0.8 maximum_maximum_fusion
  2.2 7.6 %all_gather.3.ctx_ref = bf16[640,256]{1,0:T(8,128)(2,1)S(1)} all-gather(bf16[160,256]{1,0:T(8,128)(2,1)S(1)} %maximum_maximum_fusion), channel_id=1, replica_groups=mesh['seq'=4,'head'=8] {'seq'}, dimensions={0}, use_global_device_ids=true | all-gather | bytes 409600 | tf_op jit(solution)/shard_map/all_gather | solution.py:187
  9.7 0.0 copy-start
  9.7 0.9 copy-done
  10.7 0.0 copy-start.1
  10.7 0.8 copy-done.1
  11.4 0.0 copy-start.2
  11.4 0.8 copy-done.2
  12.2 0.0 copy-start.3
  12.2 0.7 copy-done.3
  12.9 14.0 %attention.1 = bf16[128,1024]{1,0:T(8,128)(2,1)S(1)} custom-call(s32[1]{0:T(128)} %bitcast.own_ref, s32[1]{0:T(128)} %bitcast.1.base_ref, s32[128]{0:T(128)S(1)} %copy-done.3, bf16[128,1024]{1,0:T(8,128)(2,1)S(1)} %copy-done, bf16[640,256]{1,0:T(8,128)(2,1)S(1)} %all_gather.3.ctx_ref, bf16[128,128]{1,0:T(8,128)(2,1)S(1)} %copy-done.2, ...), custom_call_target="tpu_custom_call" | custom-call | tf_op jit(solution)/shard_map/attention/pallas_call | solution.py:161
  26.9 4.3 %collective-permute-start = (bf16[1,128,1024]{2,1,0:T(8,128)(2,1)S(1)}, bf16[1,128,1024]{2,1,0:T(8,128)(2,1)S(1)}, u32[]{:S(2)}, u32[]{:S(2)}) collective-permute-start(bf16[1,128,1024]{2,1,0:T(8,128)(2,1)S(1)} %bitcast.29), channel_id=1, source_target_pairs={{0,16},{8,24},{16,0},{24,8},{1,17},{9,25},{17,1},{25,9},{2,18},{10... | collective-permute-start | bytes 786440 | tf_op jit(solution)/shard_map/ppermute | solution.py:203
  31.2 4.4 %collective-permute-done = bf16[1,128,1024]{2,1,0:T(8,128)(2,1)S(1)} collective-permute-done((bf16[1,128,1024]{2,1,0:T(8,128)(2,1)S(1)}, bf16[1,128,1024]{2,1,0:T(8,128)(2,1)S(1)}, u32[]{:S(2)}, u32[]{:S(2)}) %collective-permute-start) | collective-permute-done | bytes 262176 | tf_op jit(solution)/shard_map/ppermute | solution.py:203
  35.6 0.1 maximum_bitcast_fusion
  35.6 7.7 %collective-permute-start.1 = (bf16[2,128,1024]{2,1,0:T(8,128)(2,1)S(1)}, bf16[2,128,1024]{2,1,0:T(8,128)(2,1)S(1)}, u32[]{:S(2)}, u32[]{:S(2)}) collective-permute-start(bf16[2,128,1024]{2,1,0:T(8,128)(2,1)S(1)} %maximum_bitcast_fusion), channel_id=1, source_target_pairs={{0,8},{8,0},{16,24},{24,16},{1,9},{9,1},{17,25},{25,17},{2,10},{10... | collective-permute-start | bytes 1572872 | tf_op jit(solution)/shard_map/ppermute | solution.py:203
  43.3 0.0 copy-start.5
  43.3 1.5 %collective-permute-done.1 = bf16[2,128,1024]{2,1,0:T(8,128)(2,1)S(1)} collective-permute-done((bf16[2,128,1024]{2,1,0:T(8,128)(2,1)S(1)}, bf16[2,128,1024]{2,1,0:T(8,128)(2,1)S(1)}, u32[]{:S(2)}, u32[]{:S(2)}) %collective-permute-start.1) | collective-permute-done | bytes 524320 | tf_op jit(solution)/shard_map/ppermute | solution.py:203
  44.9 0.1 select_bitcast_fusion.1
  44.9 0.1 pad_maximum_fusion
  45.1 0.1 copy.11
  45.1 0.4 copy-done.5
  45.5 2.4 %convolution_convert_fusion = bf16[512,2048]{1,0:T(8,128)(2,1)S(1)} fusion(bf16[512,1024]{1,0:T(8,128)(2,1)S(1)} %bitcast.33, bf16[1024,2048]{1,0:T(8,128)(2,1)S(1)} %copy-done.5), kind=kOutput, calls=%fused_computation.1 | convolution fusion | flops 2148532224 | bytes 7340032 | tf_op jit(solution)/shard_map/dot_general | solution.py:242
  47.9 0.0 copy-start.4
  47.9 56.0 %all_to_all.5 = bf16[32,16,2048]{2,1,0:T(8,128)(2,1)S(1)} all-to-all(bf16[32,16,2048]{2,1,0:T(8,128)(2,1)S(1)} %bitcast.32), channel_id=1, replica_groups=mesh['seq'=4,'head'=8] {'seq','head'}, dimensions={0} | all-to-all | bytes 4194304 | tf_op jit(solution)/shard_map/all_to_all | solution.py:244
  103.9 0.3 convert_reduce_fusion
  104.3 0.0 copy-done.4
  104.3 0.9 add.3
  (2 shorter events, 0.1 us)
Async XLA Ops:
  9.7 0.9 copy-start
  10.7 0.8 copy-start.1
  11.4 0.8 copy-start.2
  12.2 0.7 copy-start.3
  26.9 8.6 %collective-permute-start = (bf16[1,128,1024]{2,1,0:T(8,128)(2,1)S(1)}, bf16[1,128,1024]{2,1,0:T(8,128)(2,1)S(1)}, u32[]{:S(2)}, u32[]{:S(2)}) collective-permute-start(bf16[1,128,1024]{2,1,0:T(8,128)(2,1)S(1)} %bitcast.29), channel_id=1, source_target_pairs={{0,16},{8,24},{16,0},{24,8},{1,17},{9,25},{17,1},{25,9},{2,18},{10... | collective-permute-start | bytes 786440 | tf_op jit(solution)/shard_map/ppermute | solution.py:203
  35.6 9.3 %collective-permute-start.1 = (bf16[2,128,1024]{2,1,0:T(8,128)(2,1)S(1)}, bf16[2,128,1024]{2,1,0:T(8,128)(2,1)S(1)}, u32[]{:S(2)}, u32[]{:S(2)}) collective-permute-start(bf16[2,128,1024]{2,1,0:T(8,128)(2,1)S(1)} %maximum_bitcast_fusion), channel_id=1, source_target_pairs={{0,8},{8,0},{16,24},{24,16},{1,9},{9,1},{17,25},{25,17},{2,10},{10... | collective-permute-start | bytes 1572872 | tf_op jit(solution)/shard_map/ppermute | solution.py:203
  43.3 2.2 %copy-start.5 = (bf16[1024,2048]{1,0:T(8,128)(2,1)S(1)}, bf16[1024,2048]{1,0:T(8,128)(2,1)}, u32[]{:S(2)}) copy-start(bf16[1024,2048]{1,0:T(8,128)(2,1)} %param.15) | copy-start | bytes 12582916
  47.9 56.4 %copy-start.4 = (f32[16,8192]{1,0:T(8,128)S(1)}, f32[16,8192]{1,0:T(8,128)}, u32[]{:S(2)}) copy-start(f32[16,8192]{1,0:T(8,128)} %param.14) | copy-start | bytes 1572868
where the time goes:
time: 106 us; the launch traced here: 105 us
  blocking collectives  63.5 us (60%)
  Pallas kernels  14 us (13%)
  starting transfers between devices  12 us (11%)
  waiting for transfers between devices  5.89 us (6%)
  local copies, waits for them, and re-layouts  5.02 us (5%)
  matrix products  2.36 us (2%)
  other arithmetic  2.25 us (2%)
    all_to_all x1, blocking collectives, local(): lax.all_to_all(sent, ('seq', 'head'), 0, 0)  56 us
    pallas_call x1, Pallas kernels, attention(): pl.pallas_call(functools.partial(attention_kernel, first_token, count, mo...  14 us
    ppermute x2, starting transfers between devices, gathered(): other = lax.ppermute(value, 'seq', [(a, a ^ bit) for a in range(count)])  12 us
    all_gather x1, blocking collectives, context_blocks(): lax.all_gather(block, 'seq', axis=0, tiled=True)  7.55 us
    ppermute x2, waiting for transfers between devices, gathered(): other = lax.ppermute(value, 'seq', [(a, a ^ bit) for a in range(count)])  5.89 us
    unnamed x12, local copies, waits for them, and re-layouts  3.51 us
    dot_general x1, matrix products, local(): jnp.dot(every, out_weight, preferred_element_type=jnp.float32)  2.36 us
  transfers between devices with their start and end apart: 2, of which 2 were waited for; matrix products, arithmetic and copies ran while one was open for 0% of the time, Pallas kernels for 0%

commit v1 on v0

v1 whole, which is shorter than its diff:
```python
import functools
import math

import jax
import jax.numpy as jnp
from jax import lax
from jax.experimental import pallas as pl
from jax.experimental.pallas import tpu as pltpu
from jax.sharding import PartitionSpec as P

DH = 128
W1 = 512
W2 = 32
BLOCK = 128
LOW = -1e30
TILE = 8
GROUP = 4
GROUPS = 2
ROWS = TILE * W2


def attention_kernel(
    token_at, skip, steps, most, tok, own_ref, base_ref, first_ref, q_hbm, ctx_hbm, *rest,
    held,
):
    if held:
        w_hbm, out_ref, w_out, *rest = rest
    else:
        out_ref, *rest = rest
    q_ref, ctx_ref, qf, of, pkf, pk2, pvb, kx, vx, lhs, scores, weights, arrived = rest
    copies = [
        pltpu.make_async_copy(source, target, arrived.at[index])
        for index, (source, target) in enumerate(
            [(ctx_hbm, ctx_ref), (q_hbm, q_ref)]
        )
    ]
    if held:
        weight = pltpu.make_async_copy(w_hbm, w_out, arrived.at[2])
        weight.start()
    for copy in copies:
        copy.start()
    unit = GROUP * ROWS
    row = lax.broadcasted_iota(jnp.int32, (unit, DH), 0)
    col = lax.broadcasted_iota(jnp.int32, (unit, DH), 1)
    pick = jnp.where(row // TILE == col, 1.0, 0.0).astype(jnp.bfloat16)
    for g in range(GROUPS):
        lhs[g * unit : (g + 1) * unit, DH:] = pick
    for copy in copies:
        copy.wait()
    blocks = kx.shape[1] // BLOCK
    own = own_ref[0]
    base = base_ref[0]
    origin = base - own * tok
    for b in range(blocks):
        rows = slice(b * BLOCK, (b + 1) * BLOCK)
        for g in range(GROUPS):
            kx[g, rows, :DH] = ctx_ref[rows, :DH]
        vx[rows, :DH] = ctx_ref[rows, DH : 2 * DH]
        vx[rows, DH:] = jnp.ones((BLOCK, DH), jnp.bfloat16)
    before = pl.multiple_of(jnp.maximum(own * tok - W2, 0), W2)
    pkf[0:W2] = ctx_ref[pl.ds(before, W2), 2 * DH :].astype(jnp.float32)
    pkf[W2 : W2 + tok] = ctx_ref[pl.ds(pl.multiple_of(own * tok, BLOCK), tok), 2 * DH :].astype(jnp.float32)
    pkf[W2 + tok :] = jnp.zeros((8, 2 * DH), jnp.float32)

    def spread(blk, _):
        r0 = pl.multiple_of(blk * 8, 8)
        x = pkf[pl.ds(r0, 16)]
        for r in range(8):
            a = jnp.broadcast_to(x[r : r + 1, :DH], (TILE, DH))
            b = jnp.broadcast_to(x[r + 1 : r + 2, :DH], (TILE, DH))
            pk2[r0 + r] = jnp.concatenate([a, b], axis=0).astype(jnp.bfloat16)
            pvb[r0 + r] = jnp.broadcast_to(x[r : r + 1, DH:], (TILE, DH))
        return 0

    lax.fori_loop(0, (W2 + tok) // 8, spread, 0)
    for h in range(TILE):
        qf[pl.ds(h, tok, stride=TILE), :] = q_ref[:, h * DH : (h + 1) * DH].astype(jnp.float32)
    lane = lax.broadcasted_iota(jnp.int32, (1, DH), 1)
    lane_token = lane // W2
    lane_offset = lane % W2
    factor = math.log2(math.e) / math.sqrt(DH)
    tokens = GROUP * GROUPS

    def step(index, _):
        i0 = token_at + index * skip
        pos0 = base + i0
        first = [first_ref[i0 + t] for t in range(tokens)]
        lowest = jnp.maximum(first[0], pos0 - W1 + 1)
        block_low = (lowest - origin) // BLOCK
        block_high = (pos0 + tokens - 1 - origin) // BLOCK
        start = pl.multiple_of(block_low * BLOCK, BLOCK)

        def run(n):
            keys = n * BLOCK
            key_pos = lax.broadcasted_iota(jnp.int32, (keys, DH), 0) + (origin + start)

            def score(g):
                mine = first[g * GROUP : (g + 1) * GROUP]
                first_lane = jnp.full((1, DH), mine[-1], jnp.int32)
                for t in range(GROUP - 2, -1, -1):
                    first_lane = jnp.where(lane_token == t, mine[t], first_lane)
                high = pos0 + g * GROUP + lane_token
                low = jnp.maximum(first_lane, high - W1 + 1)
                low = jnp.where(high - (W2 - 1) + lane_offset >= first_lane, low, 2**30)
                ok = (key_pos >= low) & (key_pos <= high)
                kx[g, pl.ds(start, keys), DH:] = jnp.where(ok, 0.0, LOW).astype(jnp.bfloat16)
                for t in range(g * GROUP, (g + 1) * GROUP):
                    q = qf[pl.ds(pl.multiple_of((i0 + t) * TILE, TILE), TILE)]
                    q = jnp.concatenate([q, q], axis=0).astype(jnp.bfloat16)
                    for k in range(W2 // 2):
                        at = t * ROWS + k * 16
                        lhs[at : at + 16, :DH] = q * pk2[i0 + t + 1 + 2 * k]
                scores[g * unit : (g + 1) * unit, :keys] = lax.dot_general(
                    lhs[g * unit : (g + 1) * unit],
                    kx[g, pl.ds(start, keys)],
                    (((1,), (1,)), ((), ())),
                    preferred_element_type=jnp.float32,
                )

            def soften(g):
                for t in range(g * GROUP, (g + 1) * GROUP):
                    rows = slice(t * ROWS, (t + 1) * ROWS)
                    s = scores[rows, :keys].reshape(W2, TILE, keys)
                    top = jnp.max(jnp.max(s, axis=0), axis=1, keepdims=True)
                    e = jnp.exp2((s - top[None]) * factor)
                    weights[rows, :keys] = e.reshape(ROWS, keys).astype(jnp.bfloat16)

            def value(g):
                o = jnp.dot(
                    weights[g * unit : (g + 1) * unit, :keys],
                    vx[pl.ds(start, keys)],
                    preferred_element_type=jnp.float32,
                )
                for t in range(GROUP):
                    carried = jnp.zeros((TILE, DH), jnp.float32)
                    total = jnp.zeros((TILE, DH), jnp.float32)
                    for w in range(W2):
                        at = t * ROWS + w * TILE
                        carried += o[at : at + TILE, :DH] * pvb[i0 + g * GROUP + t + 1 + w]
                        total += o[at : at + TILE, DH:]
                    at = pl.multiple_of((index * tokens + g * GROUP + t) * TILE, TILE)
                    of[pl.ds(at, TILE)] = carried / total

            score(0)
            for g in range(GROUPS):
                if g + 1 < GROUPS:
                    score(g + 1)
                soften(g)
                if g >= 1:
                    value(g - 1)
            value(GROUPS - 1)

        for n in range(1, most + 1):
            pl.when(block_high - block_low + 1 == n)(functools.partial(run, n))
        return 0

    lax.fori_loop(0, steps, step, 0)
    count = steps * tokens
    for h in range(TILE):
        out_ref[:, h * DH : (h + 1) * DH] = of[pl.ds(h, count, stride=TILE), :].astype(jnp.bfloat16)
    if held:
        weight.wait()


def attention(token_at, skip, steps, own, base, first_key, q, context, held=None):
    tok = first_key.shape[0]
    count = steps * GROUP * GROUPS
    rows = context.shape[0]
    most = min(rows // BLOCK, W1 // BLOCK + 1)
    f32, bf16 = jnp.float32, jnp.bfloat16
    unit = GROUPS * GROUP * ROWS
    more = [] if held is None else [held]
    out = pl.pallas_call(
        functools.partial(attention_kernel, token_at, skip, steps, most, tok, held=held is not None),
        out_shape=[jax.ShapeDtypeStruct((count, TILE * DH), bf16)]
        + [jax.ShapeDtypeStruct(value.shape, value.dtype) for value in more],
        in_specs=[pl.BlockSpec(memory_space=pltpu.SMEM)] * 3
        + [pl.BlockSpec(memory_space=pl.ANY)] * (2 + len(more)),
        out_specs=[pl.BlockSpec(memory_space=pltpu.VMEM)]
        + [pl.BlockSpec(memory_space=pl.ANY) for value in more],
        scratch_shapes=[
            pltpu.VMEM(q.shape, bf16),
            pltpu.VMEM(context.shape, bf16),
            pltpu.VMEM((tok * TILE, DH), f32),
            pltpu.VMEM((count * TILE, DH), f32),
            pltpu.VMEM((W2 + tok + 8, 2 * DH), f32),
            pltpu.VMEM((W2 + tok, 2 * TILE, DH), bf16),
            pltpu.VMEM((W2 + tok, TILE, DH), f32),
            pltpu.VMEM((GROUPS, rows, 2 * DH), bf16),
            pltpu.VMEM((rows, 2 * DH), bf16),
            pltpu.VMEM((unit, 2 * DH), bf16),
            pltpu.VMEM((unit, most * BLOCK), f32),
            pltpu.VMEM((unit, most * BLOCK), bf16),
            pltpu.SemaphoreType.DMA((3,)),
        ],
        cost_estimate=pl.CostEstimate(
            flops=4 * count * ROWS * most * BLOCK * 2 * DH, bytes_accessed=2**20, transcendentals=0
        ),
        compiler_params=pltpu.CompilerParams(vmem_limit_bytes=24 * 2**20),
        name="attention",
    )(own, base, first_key, q, context, *more)
    return out if more else out[0]


def project_kernel(order, me_ref, kept_ref, came_ref, w_ref, out_ref, rows_ref):
    count = kept_ref.shape[1]
    pieces = [kept_ref[i] for i in range(kept_ref.shape[0])]
    pieces += [came_ref[i] for i in range(came_ref.shape[0])]
    for other, piece in zip(order, pieces, strict=True):
        at = pl.multiple_of((me_ref[0] ^ other) * count, count)
        rows_ref[pl.ds(at, count)] = piece
    columns = w_ref.shape[1]
    width = math.gcd(columns, 512)
    for at in range(0, columns, width):
        out_ref[:, at : at + width] = jnp.dot(
            rows_ref[...], w_ref[:, at : at + width], preferred_element_type=jnp.float32
        ).astype(jnp.bfloat16)


def project(features, out_weight):
    size = lax.axis_size("seq")
    me = lax.axis_index("seq").astype(jnp.int32).reshape(1)
    kept, order, bit = features[None], [0], size // 2
    while bit:
        came = lax.ppermute(kept, "seq", [(a, a ^ bit) for a in range(size)])
        order = order + [other ^ bit for other in order]
        bit //= 2
        if bit:
            kept = jnp.concatenate([kept, came], axis=0)
    rows = size * features.shape[0]
    depth, columns = out_weight.shape
    return pl.pallas_call(
        functools.partial(project_kernel, order),
        out_shape=jax.ShapeDtypeStruct((rows, columns), jnp.bfloat16),
        in_specs=[
            pl.BlockSpec(memory_space=pltpu.SMEM),
            pl.BlockSpec(memory_space=pltpu.VMEM),
            pl.BlockSpec(memory_space=pltpu.VMEM),
            pl.BlockSpec(memory_space=pltpu.VMEM),
        ],
        out_specs=pl.BlockSpec(memory_space=pltpu.VMEM),
        scratch_shapes=[pltpu.VMEM((rows, depth), jnp.bfloat16)],
        cost_estimate=pl.CostEstimate(
            flops=2 * rows * depth * columns, bytes_accessed=2 * depth * columns, transcendentals=0
        ),
        compiler_params=pltpu.CompilerParams(vmem_limit_bytes=20 * 2**20),
        name="project",
    )(me, kept, came, out_weight)


def context_blocks(block, reach):
    count = lax.axis_size("seq")
    if count <= reach + 1:
        return lax.all_gather(block, "seq", axis=0, tiled=True), lax.axis_index("seq")
    pieces = [
        lax.ppermute(block, "seq", [(a, a + steps) for a in range(count - steps)])
        for steps in range(reach, 0, -1)
    ]
    return jnp.concatenate(pieces + [block], axis=0), jnp.int32(reach)


def local(queries, key_rows, value_rows, pair_keys, pair_values, first_key, residual, out_weight):
    tok = queries.shape[0]
    width = queries.shape[1]
    seq_size, head_size = lax.axis_size("seq"), lax.axis_size("head")
    block = jnp.concatenate([key_rows, value_rows, pair_keys, pair_values], axis=1)
    context, own = context_blocks(block, (W1 + tok - 1) // tok)
    base = lax.axis_index("seq") * tok
    own, base = (jnp.asarray(value, jnp.int32).reshape(1) for value in (own, base))
    tile = TILE * DH

    step = GROUP * GROUPS

    def attend(start, skip, steps, queries, held=None):
        parts, copied = [], None
        for at in range(0, width, tile):
            q = queries[:, at : at + tile]
            if q.shape[1] < tile:
                q = jnp.pad(q, ((0, 0), (0, tile - q.shape[1])))
            part = attention(start, skip, steps, own, base, first_key, q, context, held)
            if held is not None:
                part, copied = part
                held = None
            parts.append(part)
        features = (parts[0] if len(parts) == 1 else jnp.concatenate(parts, axis=1))[:, :width]
        return (features, copied) if copied is not None else features

    columns = out_weight.shape[1]
    rows = tok // head_size

    def product(features, count, out_weight):
        return project(features, out_weight).reshape(seq_size * head_size, count, columns)

    def exchange(sent):
        return lax.all_to_all(sent, ("seq", "head"), 0, 0)

    def total(got):
        got = got.reshape(seq_size, head_size, -1, columns).astype(jnp.float32)
        return jnp.swapaxes(jnp.sum(got, axis=1), 0, 1).reshape(-1, seq_size * columns)

    if rows != 2 * step:
        sent = product(attend(0, step, tok // step, queries), rows, out_weight)
        return residual + total(exchange(sent))
    steps = tok // rows
    first = attend(0, rows, steps, queries)
    sent = product(first, step, out_weight)
    queries, sent = lax.optimization_barrier((queries, sent))
    got_first = exchange(sent)
    second = attend(step, rows, steps, queries)
    got_second = exchange(product(second, step, out_weight))
    return residual + jnp.concatenate([total(got_first), total(got_second)], axis=0)


def solution(mesh):
    placed = (
        P("seq", "head"),
        P("seq", None),
        P("seq", None),
        P("seq", None),
        P("seq", None),
        P("seq"),
        P(("seq", "head"), None),
        P("head", "seq"),
    )
    return jax.shard_map(
        local, mesh=mesh, in_specs=placed, out_specs=P(("seq", "head"), None), check_vma=False
    )
```

time: 106 us -> 95.4 us (0.900)
  blocking collectives: 63.5 us -> 8.62 us
  waiting for transfers between devices: 5.89 us -> 47.3 us
  Pallas kernels: 14 us -> 19.8 us
  local copies, waits for them, and re-layouts: 5.02 us -> 1.63 us
  matrix products: 2.36 us -> 0 us
  starting transfers between devices: 12 us -> 14 us
    all_to_all x1 -> x0, blocking collectives: 56 us -> none  [local(): lax.all_to_all(sent, ('seq', 'head'), 0, 0)]
    all_to_all x0 -> x2, waiting for transfers between devices: none -> 35.4 us  [exchange(): return lax.all_to_all(sent, ('seq', 'head'), 0, 0)]
    all_to_all x0 -> x2, starting transfers between devices: none -> 8.37 us  [exchange(): return lax.all_to_all(sent, ('seq', 'head'), 0, 0)]
    ppermute x2 -> x4, starting transfers between devices: 12 us -> 5.67 us  [project(): came = lax.ppermute(kept, 'seq', [(a, a ^ bit) for a in range(size)])]
    ppermute x2 -> x4, waiting for transfers between devices: 5.89 us -> 11.9 us  [project(): came = lax.ppermute(kept, 'seq', [(a, a ^ bit) for a in range(size)])]
    pallas_call x1 -> x4, Pallas kernels: 14 us -> 19.8 us  [the longest x2 15.3 us: attention(): pl.pallas_call(functools.partial(attention_kernel, token_at, skip, steps,...]
    dot_general x1 -> x0, matrix products: 2.36 us -> none  [local(): jnp.dot(every, out_weight, preferred_element_type=jnp.float32)]
    unnamed x12 -> x14, local copies, waits for them, and re-layouts: 3.51 us -> 1.63 us
  transfers between devices with their start and end apart: 2 -> 6, of which waited for: 2 -> 6; matrix products, arithmetic and copies ran while one was open for 0% -> 0% of each run, Pallas kernels for 0% -> 11%
where the time goes in v1:
time: 95.4 us; the launch traced here: 93.6 us
  waiting for transfers between devices  47.3 us (50%)
  Pallas kernels  19.8 us (21%)
  starting transfers between devices  14 us (15%)
  blocking collectives  8.62 us (9%)
  other arithmetic  2.06 us (2%)
  local copies, waits for them, and re-layouts  1.63 us (2%)
    all_to_all x2, waiting for transfers between devices, exchange(): return lax.all_to_all(sent, ('seq', 'head'), 0, 0)  35.4 us
    pallas_call x2, Pallas kernels, attention(): pl.pallas_call(functools.partial(attention_kernel, token_at, skip, steps,...  15.3 us
    ppermute x4, waiting for transfers between devices, project(): came = lax.ppermute(kept, 'seq', [(a, a ^ bit) for a in range(size)])  11.9 us
    all_gather x1, blocking collectives, context_blocks(): lax.all_gather(block, 'seq', axis=0, tiled=True)  8.62 us
    all_to_all x2, starting transfers between devices, exchange(): return lax.all_to_all(sent, ('seq', 'head'), 0, 0)  8.37 us
    ppermute x4, starting transfers between devices, project(): came = lax.ppermute(kept, 'seq', [(a, a ^ bit) for a in range(size)])  5.67 us
    pallas_call x2, Pallas kernels, project(): pl.pallas_call(functools.partial(project_kernel, order), out_shape=jax.Sh...  4.57 us
  transfers between devices with their start and end apart: 6, of which 6 were waited for; matrix products, arithmetic and copies ran while one was open for 0% of the time, Pallas kernels for 11%

profile of v1, /device:TPU:0, one launch (start us, length us, event | category | flops | bytes accessed | tf_op | source)
XLA Modules:
  0.0 93.6 jit_solution(5967991377405349772)
XLA Ops:
  0.0 0.8 pad_maximum_fusion.2
  0.8 8.6 %all_gather.3.ctx_hbm = bf16[512,512]{1,0:T(8,128)(2,1)S(1)} all-gather(bf16[128,512]{1,0:T(8,128)(2,1)S(1)} %pad_maximum_fusion.2), channel_id=1, replica_groups=mesh['seq'=4,'head'=8] {'seq'}, dimensions={0}, use_global_device_ids=true | all-gather | bytes 655360 | tf_op jit(solution)/shard_map/all_gather | solution.py:254
  9.4 0.0 copy-start.2
  9.4 0.9 %copy-done.2 = bf16[128,1024]{1,0:T(8,128)(2,1)S(1)} copy-done((bf16[128,1024]{1,0:T(8,128)(2,1)S(1)}, bf16[128,1024]{1,0:T(8,128)(2,1)}, u32[]{:S(2)}) %copy-start.2) | copy-done | bytes 262168
  10.4 0.0 copy-start.4
  10.4 0.7 copy-done.4
  11.1 0.0 copy-start
  11.1 7.6 %attention.2 = bf16[64,1024]{1,0:T(8,128)(2,1)S(1)} custom-call(s32[1]{0:T(128)} %bitcast.own_ref.me_ref, s32[1]{0:T(128)} %bitcast.1.base_ref, s32[128]{0:T(128)S(1)} %copy-done.4, bf16[128,1024]{1,0:T(8,128)(2,1)S(1)} %copy-done.2, bf16[512,512]{1,0:T(8,128)(2,1)S(1)} %all_gather.3.ctx_hbm), custom_call_target="tpu_custom_call" | custom-call | flops 8589934592 | bytes 1048576 | tf_op jit(solution)/shard_map/attention/pallas_call | solution.py:173
  18.7 2.5 %collective-permute-start = (bf16[1,64,1024]{2,1,0:T(8,128)(2,1)S(1)}, bf16[1,64,1024]{2,1,0:T(8,128)(2,1)S(1)}, u32[]{:S(2)}, u32[]{:S(2)}) collective-permute-start(bf16[1,64,1024]{2,1,0:T(8,128)(2,1)S(1)} %bitcast.20), channel_id=1, source_target_pairs={{0,16},{8,24},{16,0},{24,8},{1,17},{9,25},{17,1},{25,9},{2,18},{10... | collective-permute-start | bytes 393224 | tf_op jit(solution)/shard_map/ppermute | solution.py:225
  21.2 4.0 %collective-permute-done = bf16[1,64,1024]{2,1,0:T(8,128)(2,1)S(1)} collective-permute-done((bf16[1,64,1024]{2,1,0:T(8,128)(2,1)S(1)}, bf16[1,64,1024]{2,1,0:T(8,128)(2,1)S(1)}, u32[]{:S(2)}, u32[]{:S(2)}) %collective-permute-start) | collective-permute-done | bytes 131104 | tf_op jit(solution)/shard_map/ppermute | solution.py:225
  25.3 0.2 collective-permute-start.1
  25.5 1.4 %collective-permute-done.1.came_ref = bf16[2,64,1024]{2,1,0:T(8,128)(2,1)S(1)} collective-permute-done((bf16[2,64,1024]{2,1,0:T(8,128)(2,1)S(1)}, bf16[2,64,1024]{2,1,0:T(8,128)(2,1)S(1)}, u32[]{:S(2)}, u32[]{:S(2)}) %collective-permute-start.1) | collective-permute-done | bytes 262176 | tf_op jit(solution)/shard_map/ppermute | solution.py:225
  26.9 0.0 copy-done
  26.9 2.3 %project.2 = bf16[256,2048]{1,0:T(8,128)(2,1)} custom-call(s32[1]{0:T(128)} %bitcast.own_ref.me_ref, bf16[2,64,1024]{2,1,0:T(8,128)(2,1)S(1)} %pad_maximum_fusion.kept_ref, bf16[2,64,1024]{2,1,0:T(8,128)(2,1)S(1)} %collective-permute-done.1.came_ref, bf16[1024,2048]{1,0:T(8,128)(2,1)S(1)} %copy-done), custom_call_target="tpu_custom_call" | custom-call | flops 1073741824 | bytes 4194304 | tf_op jit(solution)/shard_map/project/pallas_call | solution.py:232
  29.1 0.0 copy-start.3
  29.1 0.0 copy-start.5
  29.1 5.6 %all-to-all-start = ((bf16[32,8,2048]{2,1,0:T(8,128)(2,1)}), bf16[32,8,2048]{2,1,0:T(8,128)(2,1)S(1)}, u32[]{:S(2)}, u32[]{:S(2)}) async-start(bf16[32,8,2048]{2,1,0:T(8,128)(2,1)} %bitcast.3), calls=%async_computation | async-start | bytes 2097152 | tf_op jit(solution)/shard_map/all_to_all | solution.py:295
  34.8 0.0 copy-done.3
  34.8 0.0 copy-done.5
  34.8 0.0 copy-start.1
  34.8 7.6 %attention.3 = bf16[64,1024]{1,0:T(8,128)(2,1)S(1)} custom-call(s32[1]{0:T(128)} %bitcast.own_ref.me_ref, s32[1]{0:T(128)} %bitcast.1.base_ref, s32[128]{0:T(128)S(1)} %copy-done.5, bf16[128,1024]{1,0:T(8,128)(2,1)S(1)} %copy-done.3, bf16[512,512]{1,0:T(8,128)(2,1)S(1)} %all_gather.3.ctx_hbm), custom_call_target="tpu_custom_call" | custom-call | flops 8589934592 | bytes 1048576 | tf_op jit(solution)/shard_map/attention/pallas_call | solution.py:173
  42.4 2.4 %collective-permute-start.2 = (bf16[1,64,1024]{2,1,0:T(8,128)(2,1)S(1)}, bf16[1,64,1024]{2,1,0:T(8,128)(2,1)S(1)}, u32[]{:S(2)}, u32[]{:S(2)}) collective-permute-start(bf16[1,64,1024]{2,1,0:T(8,128)(2,1)S(1)} %bitcast.18), channel_id=1, source_target_pairs={{0,16},{8,24},{16,0},{24,8},{1,17},{9,25},{17,1},{25,9},{2,18},{10... | collective-permute-start | bytes 393224 | tf_op jit(solution)/shard_map/ppermute | solution.py:225
  44.8 5.4 %collective-permute-done.2 = bf16[1,64,1024]{2,1,0:T(8,128)(2,1)S(1)} collective-permute-done((bf16[1,64,1024]{2,1,0:T(8,128)(2,1)S(1)}, bf16[1,64,1024]{2,1,0:T(8,128)(2,1)S(1)}, u32[]{:S(2)}, u32[]{:S(2)}) %collective-permute-start.2) | collective-permute-done | bytes 131104 | tf_op jit(solution)/shard_map/ppermute | solution.py:225
  50.2 0.6 collective-permute-start.3
  50.7 1.2 %collective-permute-done.3.came_ref = bf16[2,64,1024]{2,1,0:T(8,128)(2,1)S(1)} collective-permute-done((bf16[2,64,1024]{2,1,0:T(8,128)(2,1)S(1)}, bf16[2,64,1024]{2,1,0:T(8,128)(2,1)S(1)}, u32[]{:S(2)}, u32[]{:S(2)}) %collective-permute-start.3) | collective-permute-done | bytes 262176 | tf_op jit(solution)/shard_map/ppermute | solution.py:225
  51.9 0.0 copy-done.1
  51.9 2.3 %project.3 = bf16[256,2048]{1,0:T(8,128)(2,1)} custom-call(s32[1]{0:T(128)} %bitcast.own_ref.me_ref, bf16[2,64,1024]{2,1,0:T(8,128)(2,1)S(1)} %pad_maximum_fusion.1.kept_ref, bf16[2,64,1024]{2,1,0:T(8,128)(2,1)S(1)} %collective-permute-done.3.came_ref, bf16[1024,2048]{1,0:T(8,128)(2,1)S(1)} %copy-done.1), custom_call_target="tpu_custom_call" | custom-call | flops 1073741824 | bytes 4194304 | tf_op jit(solution)/shard_map/project/pallas_call | solution.py:232
  54.2 7.9 %all-to-all-done = bf16[32,8,2048]{2,1,0:T(8,128)(2,1)S(1)} async-done(((bf16[32,8,2048]{2,1,0:T(8,128)(2,1)}), bf16[32,8,2048]{2,1,0:T(8,128)(2,1)S(1)}, u32[]{:S(2)}, u32[]{:S(2)}) %all-to-all-start) | async-done | bytes 1048608 | tf_op jit(solution)/shard_map/all_to_all | solution.py:295
  62.2 0.0 copy-start.6
  62.2 2.8 %all-to-all-start.1 = ((bf16[32,8,2048]{2,1,0:T(8,128)(2,1)}), bf16[32,8,2048]{2,1,0:T(8,128)(2,1)S(1)}, u32[]{:S(2)}, u32[]{:S(2)}) async-start(bf16[32,8,2048]{2,1,0:T(8,128)(2,1)} %bitcast.8), calls=%async_computation.1 | async-start | bytes 2097152 | tf_op jit(solution)/shard_map/all_to_all | solution.py:295
  64.9 0.2 convert_reduce_fusion.1
  65.1 27.4 %all-to-all-done.1 = bf16[32,8,2048]{2,1,0:T(8,128)(2,1)S(1)} async-done(((bf16[32,8,2048]{2,1,0:T(8,128)(2,1)}), bf16[32,8,2048]{2,1,0:T(8,128)(2,1)S(1)}, u32[]{:S(2)}, u32[]{:S(2)}) %all-to-all-start.1) | async-done | bytes 1048608 | tf_op jit(solution)/shard_map/all_to_all | solution.py:295
  92.5 0.2 convert_reduce_fusion
  92.7 0.0 copy-done.6
  92.7 0.9 maximum_add_fusion
  (2 shorter events, 0.1 us)
Async XLA Ops:
  9.4 0.9 %copy-start.2 = (bf16[128,1024]{1,0:T(8,128)(2,1)S(1)}, bf16[128,1024]{1,0:T(8,128)(2,1)}, u32[]{:S(2)}) copy-start(bf16[128,1024]{1,0:T(8,128)(2,1)} %q_hbm.2) | copy-start | bytes 786436
  10.4 0.7 copy-start.4
  11.1 15.8 %copy-start = (bf16[1024,2048]{1,0:T(8,128)(2,1)S(1)}, bf16[1024,2048]{1,0:T(8,128)(2,1)}, u32[]{:S(2)}) copy-start(bf16[1024,2048]{1,0:T(8,128)(2,1)} %w_ref.3) | copy-start | bytes 12582916
  18.7 6.6 %collective-permute-start = (bf16[1,64,1024]{2,1,0:T(8,128)(2,1)S(1)}, bf16[1,64,1024]{2,1,0:T(8,128)(2,1)S(1)}, u32[]{:S(2)}, u32[]{:S(2)}) collective-permute-start(bf16[1,64,1024]{2,1,0:T(8,128)(2,1)S(1)} %bitcast.20), channel_id=1, source_target_pairs={{0,16},{8,24},{16,0},{24,8},{1,17},{9,25},{17,1},{25,9},{2,18},{10... | collective-permute-start | bytes 393224 | tf_op jit(solution)/shard_map/ppermute | solution.py:225
  25.3 1.6 %collective-permute-start.1 = (bf16[2,64,1024]{2,1,0:T(8,128)(2,1)S(1)}, bf16[2,64,1024]{2,1,0:T(8,128)(2,1)S(1)}, u32[]{:S(2)}, u32[]{:S(2)}) collective-permute-start(bf16[2,64,1024]{2,1,0:T(8,128)(2,1)S(1)} %pad_maximum_fusion.kept_ref), channel_id=1, source_target_pairs={{0,8},{8,0},{16,24},{24,16},{1,9},{9,1},{17,25},{25,17},{2,10},{10... | collective-permute-start | bytes 786440 | tf_op jit(solution)/shard_map/ppermute | solution.py:225
  29.1 5.6 %copy-start.3 = (bf16[128,1024]{1,0:T(8,128)(2,1)S(1)}, bf16[128,1024]{1,0:T(8,128)(2,1)}, u32[]{:S(2)}) copy-start(bf16[128,1024]{1,0:T(8,128)(2,1)} %q_hbm.2) | copy-start | bytes 786436
  29.1 5.6 %copy-start.5 = (s32[128]{0:T(128)S(1)}, s32[128]{0:T(128)}, u32[]{:S(2)}) copy-start(s32[128]{0:T(128)} %first_ref.3) | copy-start | bytes 1540
  29.1 33.0 %all-to-all-start = ((bf16[32,8,2048]{2,1,0:T(8,128)(2,1)}), bf16[32,8,2048]{2,1,0:T(8,128)(2,1)S(1)}, u32[]{:S(2)}, u32[]{:S(2)}) async-start(bf16[32,8,2048]{2,1,0:T(8,128)(2,1)} %bitcast.3), calls=%async_computation | async-start | bytes 2097152 | tf_op jit(solution)/shard_map/all_to_all | solution.py:295
  34.8 17.1 %copy-start.1 = (bf16[1024,2048]{1,0:T(8,128)(2,1)S(1)}, bf16[1024,2048]{1,0:T(8,128)(2,1)}, u32[]{:S(2)}) copy-start(bf16[1024,2048]{1,0:T(8,128)(2,1)} %w_ref.3) | copy-start | bytes 12582916
  42.4 7.7 %collective-permute-start.2 = (bf16[1,64,1024]{2,1,0:T(8,128)(2,1)S(1)}, bf16[1,64,1024]{2,1,0:T(8,128)(2,1)S(1)}, u32[]{:S(2)}, u32[]{:S(2)}) collective-permute-start(bf16[1,64,1024]{2,1,0:T(8,128)(2,1)S(1)} %bitcast.18), channel_id=1, source_target_pairs={{0,16},{8,24},{16,0},{24,8},{1,17},{9,25},{17,1},{25,9},{2,18},{10... | collective-permute-start | bytes 393224 | tf_op jit(solution)/shard_map/ppermute | solution.py:225
  50.2 1.7 %collective-permute-start.3 = (bf16[2,64,1024]{2,1,0:T(8,128)(2,1)S(1)}, bf16[2,64,1024]{2,1,0:T(8,128)(2,1)S(1)}, u32[]{:S(2)}, u32[]{:S(2)}) collective-permute-start(bf16[2,64,1024]{2,1,0:T(8,128)(2,1)S(1)} %pad_maximum_fusion.1.kept_ref), channel_id=1, source_target_pairs={{0,8},{8,0},{16,24},{24,16},{1,9},{9,1},{17,25},{25,17},{2,10},{10... | collective-permute-start | bytes 786440 | tf_op jit(solution)/shard_map/ppermute | solution.py:225
  62.2 30.5 %copy-start.6 = (f32[16,8192]{1,0:T(8,128)S(1)}, f32[16,8192]{1,0:T(8,128)}, u32[]{:S(2)}) copy-start(f32[16,8192]{1,0:T(8,128)} %param.14) | copy-start | bytes 1572868
  62.2 30.4 %all-to-all-start.1 = ((bf16[32,8,2048]{2,1,0:T(8,128)(2,1)}), bf16[32,8,2048]{2,1,0:T(8,128)(2,1)S(1)}, u32[]{:S(2)}, u32[]{:S(2)}) async-start(bf16[32,8,2048]{2,1,0:T(8,128)(2,1)} %bitcast.8), calls=%async_computation.1 | async-start | bytes 2097152 | tf_op jit(solution)/shard_map/all_to_all | solution.py:295
